TPU v7x, 256 devices: a whole 4x4x8 slice. The times are simulated.
256 devices in a mesh: dp: 4 (over z_lo), tile: 64 (over z_hi, x, y, core).
Axes of the slice: x: 4, y: 4, z: 8 (z_hi: 2, z_lo: 4; z = z_hi * 4 + z_lo), core: 2. Of those that a mesh axis runs over, the one named last changes fastest.
Arguments:
- query: bfloat16 [4, 24576, 1536], P('dp', 'tile'), may hold values from -6 to 6
- key: bfloat16 [4, 24576, 1536], P('dp', 'tile'), may hold values from -6 to 6
- value: bfloat16 [4, 24576, 1536], P('dp', 'tile'), may hold values from -6 to 6
- text_key: bfloat16 [4, 128, 1536], P('dp', 'tile'), may hold values from -6 to 6
- text_value: bfloat16 [4, 128, 1536], P('dp', 'tile'), may hold values from -6 to 6
- text_len: int32 [4], P('dp'), may hold values from 17 to 128
- window: int32 [4, 64, 2], P('dp'), may hold values 0 or 1
- query_gain: float32 [128], replicated, may hold values from 0.5 to 3
- key_gain: float32 [128], replicated, may hold values from 0.5 to 3
- grad_out: bfloat16 [4, 24576, 1536], P('dp', 'tile'), may hold values from -6 to 6
Outputs:
- attended: bfloat16 [4, 24576, 1536], P('dp', 'tile')
- grad_query: bfloat16 [4, 24576, 1536], P('dp', 'tile')
- grad_key: bfloat16 [4, 24576, 1536], P('dp', 'tile')
- grad_value: bfloat16 [4, 24576, 1536], P('dp', 'tile')
- grad_text_key: float32 [4, 128, 1536], P('dp', 'tile')
- grad_text_value: float32 [4, 128, 1536], P('dp', 'tile')
- grad_query_gain: float32 [128], replicated
- grad_key_gain: float32 [128], replicated
All inputs are finite; a program needn't handle non-finite values. No bound on the sum of `window` on one device may be relied on, other than what follows from the above.
Results may differ from a plain program's by a relative error of at most 0.012.
The roundings to bfloat16 on the way count: a program that leaves them out, or rounds other values in their place, can miss the bound.
Values may be sent and summed in bfloat16 or wider, within the bound.
No kernel may reach another device: no remote copies, remote signals or barrier semaphores. Data moves between devices by JAX's collectives and lax.ppermute only.
A program may use at most 128 MiB of HBM per device.

v0:
```python
import jax
import jax.numpy as jnp
from jax import lax
from jax.sharding import PartitionSpec as P

HEADS = 12
HEAD = 128


def extended_2(shard, sides, width):
    for axis, dim in sides:
        peers, length = (lax.axis_size(axis), shard.shape[dim])
        up = [(i, (i + 1) % peers) for i in range(peers - 1)]
        down = [(j, i) for i, j in up]
        last = lax.slice_in_dim(shard, length - width, length, axis=dim)
        first = lax.slice_in_dim(shard, 0, width, axis=dim)
        before = lax.ppermute(last, axis, up)
        after = lax.ppermute(first, axis, down)
        shard = jnp.concatenate([before, shard, after], axis=dim)
    return shard


def from_behind(shard, axis, by):
    peers = lax.axis_size(axis)
    pairs = [(i, i + by) for i in range(peers) if 0 <= i + by < peers]
    return lax.ppermute(shard, axis, pairs)


def normed(x, gain):
    count = x.shape[0]
    values = x.astype(jnp.float32).reshape(count, HEADS, HEAD)
    inverse = lax.rsqrt(jnp.mean(values * values, -1, keepdims=True) + 1e-06)
    return ((values * inverse * gain).astype(jnp.bfloat16).reshape(count, -1), values, inverse)


def norm_back(values, inverse, gain, grad):
    count = values.shape[0]
    grad = grad.reshape(count, HEADS, HEAD)
    scaled = grad * gain
    dx = inverse * scaled - values * inverse**3 * jnp.mean(scaled * values, -1, keepdims=True)
    return (dx.reshape(count, -1), jnp.sum(grad * values * inverse, (0, 1)))


def heads_first(x):
    return x.reshape(x.shape[0], HEADS, HEAD).transpose(1, 0, 2)


def heads_last(x):
    return x.transpose(1, 0, 2).reshape(x.shape[1], -1)


def head_forward(qh, kh, vh, keep):
    scale = HEAD ** (-0.5)
    scores = jnp.dot(qh, kh.T, preferred_element_type=jnp.float32) * scale
    scores = jnp.where(keep[None, :], scores, -1e30)
    top = jnp.max(scores, -1, keepdims=True)
    expo = jnp.exp(scores - top)
    total = jnp.sum(expo, -1, keepdims=True)
    probs = (expo / total).astype(jnp.bfloat16)
    out = jnp.dot(probs, vh, preferred_element_type=jnp.float32)
    return (out, top[:, 0] + jnp.log(total[:, 0]))


def head_grads(qh, kh, vh, doh, lse, delta, allow):
    scale = HEAD ** (-0.5)
    scores = jnp.dot(qh, kh.T, preferred_element_type=jnp.float32) * scale
    scores = jnp.where(allow, scores, -1e30)
    pfull = jnp.exp(scores - lse[:, None])
    dprob = jnp.dot(doh, vh.T, preferred_element_type=jnp.float32)
    dscore = (pfull * (dprob - delta[:, None]) * scale).astype(jnp.bfloat16)
    result = ()
    result = result + (jnp.dot(dscore, kh, preferred_element_type=jnp.float32),)
    probs = pfull.astype(jnp.bfloat16)
    result = result + (
        jnp.dot(dscore.T, qh, preferred_element_type=jnp.float32),
        jnp.dot(probs.T, doh, preferred_element_type=jnp.float32),
    )
    return result


def block_grads(qh, kh, vh, doh, lse, delta, keep_rows, keep_cols):
    allow = keep_rows[:, None] & keep_cols[None, :]
    return lax.map(
        lambda a: head_grads(a[0], a[1], a[2], a[3], a[4], a[5], allow),
        (qh, kh, vh, doh, lse, delta),
    )


def per_device(
    query, key, value, text_key, text_value, text_len, window, query_gain, key_gain, grad_out
):
    rows = query.shape[1]
    place = lax.axis_index("tile")
    count = lax.axis_size("tile")
    qn, qvals, qinv = normed(query[0], query_gain)
    kn, kvals, kinv = normed(key[0], key_gain)
    tn, tvals, tinv = normed(text_key[0], key_gain)
    extended = extended_2(jnp.stack([kn, value[0]]), (("tile", 1),), rows)
    text_keys, text_vals = (
        lax.all_gather(tn, "tile", axis=0, tiled=True),
        lax.all_gather(text_value[0], "tile", axis=0, tiled=True),
    )
    text_count = text_keys.shape[0]
    bits = window[0]
    own_bits = lax.dynamic_index_in_dim(bits, place, 0, keepdims=False)
    left_ok = (own_bits[0] > 0) & (place > 0)
    right_ok = (own_bits[1] > 0) & (place < count - 1)
    own = jnp.ones((rows,), bool)
    tile_keep = jnp.concatenate(
        [jnp.broadcast_to(left_ok, (rows,)), own, jnp.broadcast_to(right_ok, (rows,))]
    )
    text_ok = jnp.arange(text_count) < text_len[0]
    keep = jnp.concatenate([tile_keep, text_ok])
    keys = jnp.concatenate([extended[0], text_keys], 0)
    vals = jnp.concatenate([extended[1], text_vals], 0)
    qh, kh, vh, doh = (
        heads_first(qn),
        heads_first(keys),
        heads_first(vals),
        heads_first(grad_out[0]),
    )
    out, lse = lax.map(lambda a: head_forward(a[0], a[1], a[2], keep), (qh, kh, vh))
    attended = heads_last(out).astype(jnp.bfloat16)
    delta = jnp.sum(doh.astype(jnp.float32) * heads_first(attended).astype(jnp.float32), -1)
    span = 3 * rows
    dq, dk, dv = block_grads(qh, kh, vh, doh, lse, delta, own, keep)
    dk, dv = (heads_last(dk), heads_last(dv))
    lower = from_behind(jnp.stack([dk[:rows], dv[:rows]]).astype(jnp.bfloat16), "tile", -1).astype(
        jnp.float32
    )
    upper = from_behind(
        jnp.stack([dk[2 * rows : span], dv[2 * rows : span]]).astype(jnp.bfloat16), "tile", 1
    ).astype(jnp.float32)
    dkn = dk[rows : 2 * rows] + lower[0] + upper[0]
    dvn = dv[rows : 2 * rows] + lower[1] + upper[1]
    dtk, dtv = (dk[span:], dv[span:])
    dqn = heads_last(dq)
    text_dk, text_dv = (
        lax.psum_scatter(dtk, "tile", scatter_dimension=0, tiled=True),
        lax.psum_scatter(dtv, "tile", scatter_dimension=0, tiled=True),
    )
    grad_query, gain_q = norm_back(qvals, qinv, query_gain, dqn)
    grad_key, gain_k = norm_back(kvals, kinv, key_gain, dkn)
    grad_text_key, gain_t = norm_back(tvals, tinv, key_gain, text_dk)
    total_q, total_k = lax.psum((gain_q, gain_k + gain_t), ("dp", "tile"))
    return (
        attended[None],
        grad_query.astype(jnp.bfloat16)[None],
        grad_key.astype(jnp.bfloat16)[None],
        dvn.astype(jnp.bfloat16)[None],
        grad_text_key[None],
        text_dv[None],
        total_q,
        total_k,
    )


def solution(mesh):
    in_specs = (
        P("dp", "tile", None),
        P("dp", "tile", None),
        P("dp", "tile", None),
        P("dp", "tile", None),
        P("dp", "tile", None),
        P("dp"),
        P("dp", None, None),
        P(),
        P(),
        P("dp", "tile", None),
    )
    out_specs = (
        P("dp", "tile", None),
        P("dp", "tile", None),
        P("dp", "tile", None),
        P("dp", "tile", None),
        P("dp", "tile", None),
        P("dp", "tile", None),
        P(),
        P(),
    )
    return jax.shard_map(
        per_device, mesh=mesh, in_specs=in_specs, out_specs=out_specs, check_vma=False
    )
```

profile of v0, /device:TPU:31, one launch (start us, length us, event | category | flops | bytes accessed | tf_op | source)
XLA Modules:
  0.0 1437.8 jit_solution(9173061517443999185)
XLA Ops:
  14.8 9.1 collective-permute-start
  29.7 129.3 %all-gather.1 = bf16[64,2,1536]{2,1,0:T(2,128)(2,1)S(1)} all-gather(bf16[1,2,1536]{2,1,0:T(2,128)(2,1)S(1)} %fusion.64), channel_id=1, replica_groups=mesh['dp'=4,'tile'=64] {'tile'}, dimensions={0}, use_global_device_ids=true | all-gather | bytes 399360 | tf_op jit(solution)/shard_map/all_gather | solution.py:100
  160.5 112.5 %all-gather = bf16[1,128,1536]{2,0,1:T(2,128)(2,1)S(1)} all-gather(bf16[1,2,1536]{2,0,1:T(2,128)(2,1)S(1)} %copy.82), channel_id=2, replica_groups=mesh['dp'=4,'tile'=64] {'tile'}, dimensions={1}, use_global_device_ids=true | all-gather | bytes 399360 | tf_op jit(solution)/shard_map/all_gather | solution.py:101
  279.3 2.4 copy.84
  281.7 2.4 copy.88
  285.3 3.3 pad_maximum_fusion
  288.6 2.4 fusion.67
  293.2 6.3 copy.85
  299.5 4.2 maximum_bitcast_fusion.1
  303.8 6.3 copy.86
  310.1 66.7 %while.29 = (s32[]{:T(128)}, bf16[12,384,128]{1,2,0:T(8,128)(2,1)}, f32[12,384]{1,0:T(8,128)}, pred[1280]{0:T(1024)(128)(4,1)S(1)}, bf16[12,384,128]{2,1,0:T(8,1...) while((s32[]{:T(128)}, bf16[12,384,128]{1,2,0:T(8,128)(2,1)}, ...), condition=%wide.region_6.7_spmd.clone, body=%wide.region_3.6_spmd.sunk.clone | while | flops 255590016 | bytes 6870353 | solution.py:122
  319.0 2.2 fusion.116
  335.6 2.2 fusion.116
  341.2 2.2 fusion.116
  357.9 2.2 fusion.116
  378.7 121.8 %while.30 = (s32[]{:T(128)}, f32[12,384,128]{1,2,0:T(8,128)}, f32[12,1280,128]{1,2,0:T(8,128)}, f32[12,1280,128]{1,2,0:T(8,128)}, bf16[12,384,128]{2,1,0:T(8,128...) while((s32[]{:T(128)}, f32[12,384,128]{1,2,0:T(8,128)}, ...), condition=%wide.region_9.10_spmd.clone.clone, body=%wide.region_8.9_spmd.clone.sunk.clone | while | flops 633077760 | bytes 11746673 | solution.py:83
  502.9 9.6 bitcast_convert_fusion
  514.5 3.1 fusion.68
  524.6 11.8 collective-permute-start.3
  539.8 3.4 slice.96
  546.4 2.5 copy.98
  550.4 790.1 %all-reduce.6.cloned.1.call-done = (f32[128,1536]{1,0:T(8,128)}, f32[128,1536]{0,1:T(8,128)}) async-done(((f32[128,1536]{1,0:T(8,128)}, f32[128,1536]{0,1:T(8,128)}), (f32[128,1536]{1,0:T(8,128)}, f32[128,1536]{0,1:T(8,128)})) %all-reduce.6.cloned.1.call-update) | async-done | bytes 1572880
  1351.6 2.9 multiply_reduce_fusion
  1356.7 74.2 %all-reduce.2 = (f32[128]{0:T(128)}, f32[128]{0:T(128)}) all-reduce(f32[128]{0:T(128)S(1)} %copy-done.30, f32[128]{0:T(128)S(1)} %add.91), channel_id=1, replica_groups=mesh['dp'=4,'tile'=64] {'dp','tile'}, use_global_device_ids=true, to_apply=%region_16.17 | all-reduce | flops 256 | bytes 2048 | tf_op jit(solution)/shard_map/psum | solution.py:145
  (281 shorter events, 235.6 us)
Async XLA Ops:
  7.2 18.8 %copy-start = (s32[1,64,2]{1,2,0:T(2,128)S(1)}, s32[1,64,2]{1,2,0:T(2,128)}, u32[]{:S(2)}) copy-start(s32[1,64,2]{1,2,0:T(2,128)} %param.20) | copy-start | bytes 1540
  7.2 1333.3 %all-reduce.6.cloned.1.call-start = ((), (), s32[]{:S(2)}) async-start(), calls=%async_computation | async-start | bytes 3145728
  13.1 12.7 copy-start.21
  14.8 145.7 %copy-start.26 = (bf16[1,2,1536]{2,1,0:T(2,128)(2,1)S(1)}, bf16[1,2,1536]{2,1,0:T(2,128)(2,1)}, u32[]{:S(2)}) copy-start(bf16[1,2,1536]{2,1,0:T(2,128)(2,1)} %param.18) | copy-start | bytes 18436
  14.8 270.5 %collective-permute-start = (bf16[2,384,1536]{1,2,0:T(8,128)(2,1)}, bf16[2,384,1536]{1,2,0:T(8,128)(2,1)}, u32[]{:S(2)}, u32[]{:S(2)}) collective-permute-start(bf16[2,384,1536]{1,2,0:T(8,128)(2,1)} %pad_maximum_fusion.1), channel_id=1, source_target_pairs={{0,1},{1,2},{2,3},{3,4},{4,5},{5,6},{6,7},{7,8},{8,9},{9,10},{10,1... | collective-permute-start | bytes 7077896 | tf_op jit(solution)/shard_map/ppermute | solution.py:17
  23.9 261.4 %collective-permute-start.1 = (bf16[2,384,1536]{1,2,0:T(8,128)(2,1)}, bf16[2,384,1536]{1,2,0:T(8,128)(2,1)}, u32[]{:S(2)}, u32[]{:S(2)}) collective-permute-start(bf16[2,384,1536]{1,2,0:T(8,128)(2,1)} %pad_maximum_fusion.1), channel_id=1, source_target_pairs={{1,0},{2,1},{3,2},{4,3},{5,4},{6,5},{7,6},{8,7},{9,8},{10,9},{11,1... | collective-permute-start | bytes 7077896 | tf_op jit(solution)/shard_map/ppermute | solution.py:18
  25.8 3.3 copy-start.17
  272.9 4.9 copy-start.27
  293.2 6.3 copy-start.10
  519.1 3.8 copy-start.7
  519.1 3.8 copy-start.8
  520.8 824.2 %collective-permute-start.2 = (bf16[2,384,1536]{1,2,0:T(8,128)(2,1)}, bf16[2,384,1536]{1,2,0:T(8,128)(2,1)S(1)}, u32[]{:S(2)}, u32[]{:S(2)}) collective-permute-start(bf16[2,384,1536]{1,2,0:T(8,128)(2,1)} %pad_maximum_fusion.2), channel_id=1, source_target_pairs={{1,0},{2,1},{3,2},{4,3},{5,4},{6,5},{7,6},{8,7},{9,8},{10,9},{11,1... | collective-permute-start | bytes 7077896 | tf_op jit(solution)/shard_map/ppermute | solution.py:26
  522.9 13.6 copy-start.29
  522.9 15.6 %copy-start.32 = (u32[256]{0:T(256)S(1)}, u32[256]{0:T(256)}, u32[]{:S(2)}) copy-start(u32[256]{0:T(256)} %constant.88) | copy-start | bytes 3076
  524.6 820.6 %collective-permute-start.3 = (bf16[2,384,1536]{1,2,0:T(8,128)(2,1)}, bf16[2,384,1536]{1,2,0:T(8,128)(2,1)}, u32[]{:S(2)}, u32[]{:S(2)}) collective-permute-start(bf16[2,384,1536]{1,2,0:T(8,128)(2,1)} %pad_maximum_fusion.3), channel_id=1, source_target_pairs={{0,1},{1,2},{2,3},{3,4},{4,5},{5,6},{6,7},{7,8},{8,9},{9,10},{10,1... | collective-permute-start | bytes 7077896 | tf_op jit(solution)/shard_map/ppermute | solution.py:26
  539.7 3.4 copy-start.5
  539.7 3.4 copy-start.14
  539.7 3.4 copy-start.28
  548.9 794.7 %copy-start.25 = (f32[128]{0:T(128)S(1)}, f32[128]{0:T(128)}, u32[]{:S(2)}) copy-start(f32[128]{0:T(128)} %param.22) | copy-start | bytes 1540
  550.3 792.4 %copy-start.16 = (f32[1,2,12,128]{3,2,1,0:T(8,128)S(1)}, f32[1,2,12,128]{3,2,1,0:T(8,128)}, u32[]{:S(2)}) copy-start(f32[1,2,12,128]{3,2,1,0:T(8,128)} %copy-done.15) | copy-start | bytes 36868
  550.3 792.4 %copy-start.22 = (bf16[1,2,1536]{2,1,0:T(2,128)(2,1)S(1)}, bf16[1,2,1536]{2,1,0:T(2,128)(2,1)}, u32[]{:S(2)}) copy-start(bf16[1,2,1536]{2,1,0:T(2,128)(2,1)} %param.17) | copy-start | bytes 18436
  550.3 793.3 %copy-start.18 = (f32[2,12,128]{2,1,0:T(8,128)S(1)}, f32[2,12,128]{2,1,0:T(8,128)}, u32[]{:S(2)}) copy-start(f32[2,12,128]{2,1,0:T(8,128)} %copy-done.17) | copy-start | bytes 36868
  550.3 794.0 %copy-start.23 = (f32[1,2,1536]{2,1,0:T(2,128)S(1)}, f32[1,2,1536]{2,1,0:T(2,128)}, u32[]{:S(2)}) copy-start(f32[1,2,1536]{2,1,0:T(2,128)} %mul.275) | copy-start | bytes 36868
  1354.5 76.4 %copy-start.1 = (s32[1,64,2]{1,2,0:T(2,128)S(1)}, s32[1,64,2]{1,2,0:T(2,128)}, u32[]{:S(2)}) copy-start(s32[1,64,2]{1,2,0:T(2,128)} %param.20) | copy-start | bytes 1540
  (14 other events, 27.8 us)
Sparse Core Ops, SparseCore 0:
  519.2 821.2 all-reduce.5
where the time goes:
time: 1450 us; the launch traced here: 1440 us
  waiting for transfers between devices  790 us (54%)
  blocking collectives  316 us (22%)
  matrix products  158 us (11%)
  local copies, waits for them, and re-layouts  80.1 us (6%)
  other arithmetic  51 us (4%)
  starting transfers between devices  24.9 us (2%)
  between operations  17.1 us (1%)
    unnamed x2, waiting for transfers between devices  790 us
    all_gather x1, blocking collectives, per_device(): lax.all_gather(tn, 'tile', axis=0, tiled=True)  129 us
    all_gather x1, blocking collectives, per_device(): lax.all_gather(text_value[0], 'tile', axis=0, tiled=True)  112 us
    psum x1, blocking collectives, per_device(): total_q, total_k = lax.psum((gain_q, gain_k + gain_t), ('dp', 'tile'))  74.2 us
  transfers between devices with their start and end apart: 5, of which 1 were waited for; matrix products, arithmetic and copies ran while one was open for 2% of the time, Pallas kernels for 0%

commit v1 on v0

v1 whole, which is shorter than its diff:
```python
import functools
import math

import jax
import jax.numpy as jnp
from jax import lax
from jax.experimental import pallas as pl
from jax.experimental.pallas import tpu as pltpu
from jax.sharding import PartitionSpec as P

HEADS = 12
HEAD = 128
TT = 384
TXT = 128
W = HEADS * HEAD
CHUNKS = 2
PER = HEADS // CHUNKS
CW = PER * HEAD
SCALE = HEAD ** (-0.5)
BIG = 1e30
F32 = jnp.float32
BF16 = jnp.bfloat16

SIZES = (2, 4, 4, 2)


def place_of(zh, x, y, c):
    return ((zh * 4 + x) * 4 + y) * 2 + c


def steps_along(dim, by):
    pairs = []
    for i in range(64):
        at = [i // 32, i // 8 % 4, i // 2 % 4, i % 2]
        to = list(at)
        to[dim] = (at[dim] + by) % SIZES[dim]
        pairs.append((i, place_of(*to)))
    return pairs


def nt(a, b):
    return lax.dot_general(a, b, (((1,), (1,)), ((), ())), preferred_element_type=F32)


def nn(a, b):
    return lax.dot_general(a, b, (((1,), (0,)), ((), ())), preferred_element_type=F32)


def normed(x, gain):
    x = x.astype(F32)
    inv = lax.rsqrt(jnp.mean(x * x, -1, keepdims=True) + 1e-06)
    hat = x * inv
    return x, inv, hat, (hat * gain).astype(BF16)


def attend_kernel(flags, q_ref, k_ref, v_ref, g_ref, lo_ref, hi_ref, t_ref, keep_ref, qg_ref, kg_ref, *rest):
    att_ref, gq_ref, own_ref, dlo_ref, dhi_ref, dt_ref, gain_ref, s_ref, p_ref, d_ref = rest[-10:]
    step = pl.program_id(0)
    qg, kg = qg_ref[...], kg_ref[...]
    q, q_inv, q_hat, qn = normed(q_ref[...], qg)
    scaled = qn.astype(F32) * (SCALE * math.log2(math.e))
    high = scaled.astype(BF16)
    low = (scaled - high.astype(F32)).astype(BF16)
    queries = jnp.concatenate([high, low], 1)
    lower, upper = flags[0] > 0, flags[1] > 0

    raw = (lo_ref[0], k_ref[...], hi_ref[0], t_ref[0])
    vals = (lo_ref[1], v_ref[...], hi_ref[1], t_ref[1])
    starts = (0, TT, 2 * TT, 3 * TT)
    rows = (TT, TT, TT, TXT)
    hats, keys = [], []
    for x in raw:
        _, _, hat, kn = normed(x, kg)
        hats.append(hat)
        keys.append(kn)

    tops = []
    for b in range(4):
        s = nt(jnp.concatenate([keys[b], keys[b]], 1), queries)
        if b == 3:
            s = jnp.where(keep_ref[...] > 0, s, -BIG)
        s_ref[pl.ds(starts[b], rows[b]), :] = s
        top = jnp.max(s, 0, keepdims=True)
        if b == 0:
            top = jnp.where(lower, top, -BIG)
        if b == 2:
            top = jnp.where(upper, top, -BIG)
        tops.append(top)
    top = jnp.maximum(jnp.maximum(tops[0], tops[1]), jnp.maximum(tops[2], tops[3]))
    total = jnp.zeros((1, TT), F32)
    for b in range(4):
        shift = top
        if b == 0:
            shift = jnp.where(lower, top, BIG)
        if b == 2:
            shift = jnp.where(upper, top, BIG)
        e = jnp.exp2(s_ref[pl.ds(starts[b], rows[b]), :] - shift)
        s_ref[pl.ds(starts[b], rows[b]), :] = e
        total += jnp.sum(e, 0, keepdims=True)
    part = 1.0 / total
    out = jnp.zeros((HEAD, TT), F32)
    for b in range(4):
        p = s_ref[pl.ds(starts[b], rows[b]), :] * part
        s_ref[pl.ds(starts[b], rows[b]), :] = p
        p16 = p.astype(BF16)
        p_ref[pl.ds(starts[b], rows[b]), :] = p16
        out += nn(vals[b].T, p16)
    att = out.T.astype(BF16)
    att_ref[...] = att

    g = g_ref[...]
    delta = jnp.sum(g.astype(F32) * att.astype(F32), -1, keepdims=True)
    lane = lax.broadcasted_iota(jnp.int32, (TT, HEAD), 1)
    d1 = delta.astype(BF16).astype(F32)
    d2 = (delta - d1).astype(BF16).astype(F32)
    d3 = delta - d1 - d2
    extra = jnp.where(lane == 0, -d1, jnp.where(lane == 1, -d2, jnp.where(lane == 2, -d3, 0.0)))
    cot = jnp.concatenate([g, extra.astype(BF16)], 1)
    dq = jnp.zeros((HEAD, TT), F32)
    gain_k = jnp.zeros((1, HEAD), F32)
    for b in range(4):
        ones = (lax.broadcasted_iota(jnp.int32, (rows[b], HEAD), 1) < 3).astype(F32).astype(BF16)
        dp = nt(jnp.concatenate([vals[b], ones], 1), cot)
        ds = (s_ref[pl.ds(starts[b], rows[b]), :] * dp).astype(BF16)
        d_ref[pl.ds(starts[b], rows[b]), :] = ds
        dq += nn(keys[b].T, ds)
        dk = nn(ds, qn) * SCALE
        dv = nn(p_ref[pl.ds(starts[b], rows[b]), :], g)
        gain_k += jnp.sum(dk * hats[b], 0, keepdims=True)
        into = (dlo_ref, own_ref, dhi_ref, dt_ref)[b]
        into[0] = dk.astype(into.dtype)
        into[1] = dv.astype(into.dtype)
    dqn = dq.T * SCALE
    u = dqn * qg
    gq_ref[...] = (q_inv * u - q_hat * (q_inv * q_inv) * jnp.mean(u * q, -1, keepdims=True)).astype(BF16)
    gain_q = jnp.sum(dqn * q_hat, 0, keepdims=True)
    row = lax.broadcasted_iota(jnp.int32, (8, HEAD), 0)
    gains = jnp.where(row == 0, gain_q, jnp.where(row == 1, gain_k, 0.0))

    @pl.when(step == 0)
    def _():
        gain_ref[...] = gains

    @pl.when(step > 0)
    def _():
        gain_ref[...] += gains


def attend(chunk, flags, q, k, v, g, lo, hi, text, keep, qg, kg, before):
    base = chunk * PER
    wide = pl.BlockSpec((TT, HEAD), lambda h, f: (0, h + base))
    pair = pl.BlockSpec((2, TT, HEAD), lambda h, f: (0, 0, h))
    tpair = pl.BlockSpec((2, TXT, HEAD), lambda h, f: (0, 0, h))
    tall = pl.BlockSpec((2, TXT, HEAD), lambda h, f: (0, 0, h + base))
    whole = lambda *shape: pl.BlockSpec(shape, lambda h, f: (0,) * len(shape))
    in_specs = [wide] * 4 + [pair, pair, tall, whole(TXT, 1), whole(1, HEAD), whole(1, HEAD)]
    args = [q, k, v, g, lo, hi, text, keep, qg, kg]
    aliases = {}
    if before is not None:
        aliases = {len(args) + 1: 0, len(args) + 2: 1}
        in_specs += [pl.BlockSpec(memory_space=pl.ANY)] * 2
        args += list(before)
    size = (3 * TT + TXT) * TT * PER
    return pl.pallas_call(
        attend_kernel,
        grid_spec=pltpu.PrefetchScalarGridSpec(
            num_scalar_prefetch=1,
            grid=(PER,),
            in_specs=in_specs,
            out_specs=[wide, wide, pair, pair, pair, tpair, whole(8, HEAD)],
            scratch_shapes=[
                pltpu.VMEM((3 * TT + TXT, TT), F32),
                pltpu.VMEM((3 * TT + TXT, TT), BF16),
                pltpu.VMEM((3 * TT + TXT, TT), BF16),
            ],
        ),
        out_shape=[
            jax.ShapeDtypeStruct((TT, W), BF16),
            jax.ShapeDtypeStruct((TT, W), BF16),
            jax.ShapeDtypeStruct((2, TT, CW), F32),
            jax.ShapeDtypeStruct((2, TT, CW), BF16),
            jax.ShapeDtypeStruct((2, TT, CW), BF16),
            jax.ShapeDtypeStruct((2, TXT, CW), F32),
            jax.ShapeDtypeStruct((8, HEAD), F32),
        ],
        input_output_aliases=aliases,
        compiler_params=pltpu.CompilerParams(vmem_limit_bytes=40 * 2**20),
        cost_estimate=pl.CostEstimate(flops=12 * 2 * HEAD * size, bytes_accessed=14 * TT * CW * 2, transcendentals=size),
    )(flags, *args)


def finish_kernel(k_ref, own_ref, a_ref, b_ref, kg_ref, *rest):
    gk_ref, gv_ref = rest[-2:]
    k, inv, hat, _ = normed(k_ref[...], kg_ref[...])
    dk = own_ref[0] + a_ref[0].astype(F32) + b_ref[0].astype(F32)
    u = dk * kg_ref[...]
    gk_ref[...] = (inv * u - hat * (inv * inv) * jnp.mean(u * k, -1, keepdims=True)).astype(BF16)
    gv_ref[...] = (own_ref[1] + a_ref[1].astype(F32) + b_ref[1].astype(F32)).astype(BF16)


def finish(chunk, k, own, a, b, kg, before):
    base = chunk * PER
    wide = pl.BlockSpec((TT, HEAD), lambda h: (0, h + base))
    pair = pl.BlockSpec((2, TT, HEAD), lambda h: (0, 0, h))
    in_specs = [wide, pair, pair, pair, pl.BlockSpec((1, HEAD), lambda h: (0, 0))]
    args = [k, own, a, b, kg]
    aliases = {}
    if before is not None:
        aliases = {len(args): 0, len(args) + 1: 1}
        in_specs += [pl.BlockSpec(memory_space=pl.ANY)] * 2
        args += list(before)
    return pl.pallas_call(
        finish_kernel,
        grid=(PER,),
        in_specs=in_specs,
        out_specs=[wide, wide],
        out_shape=[jax.ShapeDtypeStruct((TT, W), BF16)] * 2,
        input_output_aliases=aliases,
        cost_estimate=pl.CostEstimate(flops=20 * TT * CW, bytes_accessed=22 * TT * CW, transcendentals=TT),
    )(*args)


def send(x, pairs):
    return lax.ppermute(x, "tile", pairs)


def gather_text(x):
    x = x[None]
    for dim in (3, 2, 1, 0):
        got = [x] + [send(x, steps_along(dim, by)) for by in range(1, SIZES[dim])]
        x = jnp.concatenate(got, 0)
    return x


def reduce_text(x, extra):
    width = x.shape[-1]
    slots = x.reshape(64, -1)
    tail = extra.reshape(1, -1)
    for dim in (3, 1, 2, 0):
        size = SIZES[dim]
        n = slots.shape[0]
        left = [d for d in (0, 1, 2, 3) if not (dim == 1 and d == 3) and not (dim == 2 and d in (3, 1)) and not (dim == 0 and d in (3, 1, 2))]
        shape = [SIZES[d] for d in left]
        at = left.index(dim)
        view = jnp.moveaxis(slots.reshape(shape + [-1]), at, 0).reshape(size, n // size, -1)
        total, total_tail = view[0], tail
        for by in range(1, size):
            pack = jnp.concatenate([view[by].reshape(-1), tail.reshape(-1)])
            got = send(pack, steps_along(dim, -by))
            total = total + got[: total.size].reshape(total.shape)
            total_tail = total_tail + got[total.size :].reshape(tail.shape)
        slots, tail = total, total_tail
    return slots.reshape(2, width), tail.reshape(-1)


def per_device(query, key, value, text_key, text_value, text_len, window, query_gain, key_gain, grad_out):
    me = lax.axis_index("tile")
    up = [(i, i + 1) for i in range(63)]
    down = [(i + 1, i) for i in range(63)]
    q, k, v, g = query[0], key[0], value[0], grad_out[0]
    bits = lax.dynamic_index_in_dim(window[0], me, 0, keepdims=False)
    flags = jnp.stack([((bits[0] > 0) & (me > 0)).astype(jnp.int32), ((bits[1] > 0) & (me < 63)).astype(jnp.int32)])
    qg, kg = query_gain.reshape(1, HEAD), key_gain.reshape(1, HEAD)

    los, his = [], []
    for c in range(CHUNKS):
        cols = slice(c * CW, (c + 1) * CW)
        pack = jnp.stack([k[:, cols], v[:, cols]])
        los.append(send(pack, up))
        his.append(send(pack, down))

    tkv = jnp.stack([text_key[0], text_value[0]])
    tall = gather_text(tkv.reshape(-1, HEAD)).reshape(64, 2, 2, W)
    text = tall.transpose(1, 0, 2, 3).reshape(2, TXT, W)
    slot = jnp.arange(64)
    mine = (me // 32, me // 8 % 4, me // 2 % 4, me % 2)
    back = (slot // 32, slot // 8 % 4, slot // 2 % 4, slot % 2)
    owner = place_of(*[(m - b) % s for m, b, s in zip(mine, back, SIZES)])
    index = (owner[:, None] * 2 + jnp.arange(2)[None, :]).reshape(TXT, 1)
    keep = (index < text_len[0]).astype(F32)

    outs = None
    parts, gains = [], 0.0
    for c in range(CHUNKS):
        att, gq, own, dlo, dhi, dt, gain = attend(c, flags, q, k, v, g, los[c], his[c], text, keep, qg, kg, outs)
        outs = (att, gq)
        gains = gains + gain[:2]
        from_upper = send(dlo, down)
        from_lower = send(dhi, up)
        parts.append((own, from_upper, from_lower, dt))
    fins = None
    for c in range(CHUNKS):
        own, a, b, dt = parts[c]
        fins = finish(c, k, own, a, b, kg, fins)

    dt = jnp.concatenate([p[3] for p in parts], -1)
    dt = dt.reshape(2, 64, 2, W).transpose(1, 0, 2, 3).reshape(64, 1, 4 * W)
    mine_dt, gains = reduce_text(dt.reshape(64, 2, 2 * W), gains)
    total = gains
    for by in range(1, 4):
        total = total + lax.ppermute(gains, "dp", [(i, (i + by) % 4) for i in range(4)])
    mine_dt = mine_dt.reshape(2, 2, W)
    dtn, dtv = mine_dt[0], mine_dt[1]
    heads = lambda x: x.reshape(2, HEADS, HEAD)
    t = heads(text_key[0].astype(F32))
    inv = lax.rsqrt(jnp.mean(t * t, -1, keepdims=True) + 1e-06)
    u = heads(dtn) * key_gain
    gtk = (inv * u - t * inv**3 * jnp.mean(u * t, -1, keepdims=True)).reshape(2, W)
    return (
        outs[0][None],
        outs[1][None],
        fins[0][None],
        fins[1][None],
        gtk[None],
        dtv[None],
        total[:HEAD],
        total[HEAD:],
    )


def solution(mesh):
    row = P("dp", "tile", None)
    in_specs = (row, row, row, row, row, P("dp"), P("dp", None, None), P(), P(), row)
    out_specs = (row, row, row, row, row, row, P(), P())
    return jax.shard_map(per_device, mesh=mesh, in_specs=in_specs, out_specs=out_specs, check_vma=False)
```

time: 1450 us -> 294 us (0.20)
  waiting for transfers between devices: 790 us -> 81.8 us
  blocking collectives: 316 us -> 0 us
  matrix products: 158 us -> 0 us
  Pallas kernels: 0 us -> 58.3 us
  starting transfers between devices: 24.9 us -> 82.5 us
  other arithmetic: 51 us -> 14.2 us
  local copies, waits for them, and re-layouts: 80.1 us -> 52 us
    unnamed x2 -> x0, waiting for transfers between devices: 790 us -> none
    all_gather x2 -> x0, blocking collectives: 242 us -> none  [the longest x1 129 us: per_device(): lax.all_gather(tn, 'tile', axis=0, tiled=True)]
    dot_general x84 -> x0, matrix products: 158 us -> none  [the longest x12 26.7 us: head_forward(): out = jnp.dot(probs, vh, preferred_element_type=jnp.float32)]
    ppermute x4 -> x27, waiting for transfers between devices: 0.01 us -> 81.8 us  [the longest x24 48.1 us: send(): return lax.ppermute(x, 'tile', pairs)]
    psum x1 -> x0, blocking collectives: 74.2 us -> none  [per_device(): total_q, total_k = lax.psum((gain_q, gain_k + gain_t), ('dp', 'tile'))]
    pallas_call x0 -> x4, Pallas kernels: none -> 58.3 us  [the longest x2 46.9 us: attend(): pl.pallas_call(attend_kernel, grid_spec=pltpu.PrefetchScalarGridSpec(num_...]
    ppermute x4 -> x27, starting transfers between devices: 24.9 us -> 82.5 us  [the longest x24 82.4 us: send(): return lax.ppermute(x, 'tile', pairs)]
    dynamic_update_slice x12 -> x0, local copies, waits for them, and re-layouts: 15.9 us -> none  [per_device(): lax.map(lambda a: head_forward(a[0], a[1], a[2], keep), (qh, kh, vh))]
  transfers between devices with their start and end apart: 5 -> 27, of which waited for: 1 -> 12; matrix products, arithmetic and copies ran while one was open for 2% -> 12% of each run, Pallas kernels for 0% -> 10%
where the time goes in v1:
time: 294 us; the launch traced here: 292 us
  starting transfers between devices  82.5 us (28%)
  waiting for transfers between devices  81.8 us (28%)
  Pallas kernels  58.3 us (20%)
  local copies, waits for them, and re-layouts  52 us (18%)
  other arithmetic  14.2 us (5%)
  between operations  3.28 us (1%)
    ppermute x24, starting transfers between devices, send(): return lax.ppermute(x, 'tile', pairs)  82.4 us
    ppermute x24, waiting for transfers between devices, send(): return lax.ppermute(x, 'tile', pairs)  48.1 us
    pallas_call x2, Pallas kernels, attend(): pl.pallas_call(attend_kernel, grid_spec=pltpu.PrefetchScalarGridSpec(num_...  46.9 us
    ppermute x3, waiting for transfers between devices, per_device(): lax.ppermute(gains, 'dp', [(i, (i + by) % 4) for i in range(4)])  33.7 us
    unnamed x72, local copies, waits for them, and re-layouts  11.9 us
    pallas_call x2, Pallas kernels, finish(): pl.pallas_call(finish_kernel, grid=(PER,), in_specs=in_specs, out_specs=[...  11.4 us
    reshape x7, local copies, waits for them, and re-layouts, reduce_text(): total = total + got[:total.size].reshape(total.shape)  6.92 us
  transfers between devices with their start and end apart: 27, of which 12 were waited for; matrix products, arithmetic and copies ran while one was open for 12% of the time, Pallas kernels for 10%

profile of v1, /device:TPU:31, one launch (start us, length us, event | category | flops | bytes accessed | tf_op | source)
XLA Modules:
  0.0 292.1 jit_solution(14122018521209382840)
XLA Ops:
  3.5 2.6 collective-permute-start.1
  6.1 11.1 %collective-permute-start = (bf16[2,384,768]{2,1,0:T(8,128)(2,1)}, bf16[2,384,768]{2,1,0:T(8,128)(2,1)}, u32[]{:S(2)}, u32[]{:S(2)}) collective-permute-start(bf16[2,384,768]{2,1,0:T(8,128)(2,1)} %pad_maximum_fusion.1), channel_id=1, source_target_pairs={{0,1},{1,2},{2,3},{3,4},{4,5},{5,6},{6,7},{7,8},{8,9},{9,10},{10,1... | collective-permute-start | bytes 3538952 | tf_op jit(solution)/shard_map/ppermute | solution.py:224
  20.3 11.8 %collective-permute-start.10 = (bf16[2,384,768]{2,1,0:T(8,128)(2,1)}, bf16[2,384,768]{2,1,0:T(8,128)(2,1)}, u32[]{:S(2)}, u32[]{:S(2)}) collective-permute-start(bf16[2,384,768]{2,1,0:T(8,128)(2,1)} %pad_maximum_fusion.2), channel_id=1, source_target_pairs={{0,1},{1,2},{2,3},{3,4},{4,5},{5,6},{6,7},{7,8},{8,9},{9,10},{10,1... | collective-permute-start | bytes 3538952 | tf_op jit(solution)/shard_map/ppermute | solution.py:224
  35.3 2.6 collective-permute-done.3
  38.0 4.5 %collective-permute-done.4 = bf16[2,48,128]{2,1,0:T(8,128)(2,1)S(1)} collective-permute-done((bf16[2,48,128]{2,1,0:T(8,128)(2,1)S(1)}, bf16[2,48,128]{2,1,0:T(8,128)(2,1)S(1)}, u32[]{:S(2)}, u32[]{:S(2)}) %collective-permute-start.4) | collective-permute-done | bytes 24608 | tf_op jit(solution)/shard_map/ppermute | solution.py:224
  43.1 3.6 %collective-permute-done.5 = bf16[2,48,128]{2,1,0:T(8,128)(2,1)S(1)} collective-permute-done((bf16[2,48,128]{2,1,0:T(8,128)(2,1)S(1)}, bf16[2,48,128]{2,1,0:T(8,128)(2,1)S(1)}, u32[]{:S(2)}, u32[]{:S(2)}) %collective-permute-start.5) | collective-permute-done | bytes 24608 | tf_op jit(solution)/shard_map/ppermute | solution.py:224
  47.0 3.3 %collective-permute-done.6 = bf16[8,48,128]{2,1,0:T(8,128)(2,1)S(1)} collective-permute-done((bf16[8,48,128]{2,1,0:T(8,128)(2,1)S(1)}, bf16[8,48,128]{2,1,0:T(8,128)(2,1)S(1)}, u32[]{:S(2)}, u32[]{:S(2)}) %collective-permute-start.6) | collective-permute-done | bytes 98336 | tf_op jit(solution)/shard_map/ppermute | solution.py:224
  51.1 4.1 %collective-permute-done.7 = bf16[8,48,128]{2,1,0:T(8,128)(2,1)S(1)} collective-permute-done((bf16[8,48,128]{2,1,0:T(8,128)(2,1)S(1)}, bf16[8,48,128]{2,1,0:T(8,128)(2,1)S(1)}, u32[]{:S(2)}, u32[]{:S(2)}) %collective-permute-start.7) | collective-permute-done | bytes 98336 | tf_op jit(solution)/shard_map/ppermute | solution.py:224
  55.5 4.4 %collective-permute-done.8 = bf16[8,48,128]{2,1,0:T(8,128)(2,1)S(1)} collective-permute-done((bf16[8,48,128]{2,1,0:T(8,128)(2,1)S(1)}, bf16[8,48,128]{2,1,0:T(8,128)(2,1)S(1)}, u32[]{:S(2)}, u32[]{:S(2)}) %collective-permute-start.8) | collective-permute-done | bytes 98336 | tf_op jit(solution)/shard_map/ppermute | solution.py:224
  59.9 7.7 %collective-permute-start.9 = (bf16[32,48,128]{2,1,0:T(8,128)(2,1)S(1)}, bf16[32,48,128]{2,1,0:T(8,128)(2,1)S(1)}, u32[]{:S(2)}, u32[]{:S(2)}) collective-permute-start(bf16[32,48,128]{2,1,0:T(8,128)(2,1)S(1)} %constant_dynamic-update-slice_fusion.9), channel_id=1, source_target_pairs={{0,32},{1,33},{2,34},{3,35},{4,36},{5,37},{6,38},{7,39},{8,40},{9,... | collective-permute-start | bytes 1179656 | tf_op jit(solution)/shard_map/ppermute | solution.py:224
  68.0 13.9 %collective-permute-done.9 = bf16[32,48,128]{2,1,0:T(8,128)(2,1)S(1)} collective-permute-done((bf16[32,48,128]{2,1,0:T(8,128)(2,1)S(1)}, bf16[32,48,128]{2,1,0:T(8,128)(2,1)S(1)}, u32[]{:S(2)}, u32[]{:S(2)}) %collective-permute-start.9) | collective-permute-done | bytes 393248 | tf_op jit(solution)/shard_map/ppermute | solution.py:224
  88.8 23.4 %shard_map.161 = (bf16[384,1536]{1,0:T(8,128)(2,1)}, bf16[384,1536]{1,0:T(8,128)(2,1)}, f32[2,384,768]{2,1,0:T(8,128)S(1)}, bf16[2,384,768]{2,1,0:T(8,128)(2,1)S...) custom-call(s32[2]{0:T(128)S(1)} %add_convert_fusion.flags, ...), custom_call_target="tpu_custom_call" | custom-call | flops 9059696640 | bytes 8257536 | tf_op jit(solution)/shard_map/pallas_call | solution.py:164
  114.7 23.5 %shard_map.162 = (bf16[384,1536]{1,0:T(8,128)(2,1)}, bf16[384,1536]{1,0:T(8,128)(2,1)}, f32[2,384,768]{2,1,0:T(8,128)S(1)}, bf16[2,384,768]{2,1,0:T(8,128)(2,1)S...) custom-call(s32[2]{0:T(128)S(1)} %add_convert_fusion.flags, ...), custom_call_target="tpu_custom_call", output_to_operand_aliasing={{0}: (11, {}), {1}: (12, {})} | custom-call | flops 9059696640 | bytes 8257536 | tf_op jit(solution)/shard_map/pallas_call | solution.py:164
  144.1 3.4 %reshape_reshape_reshape_reshape.3 = f32[2,4,4,2,6144]{4,3,2,1,0:T(2,128)S(1)} reshape(f32[64,2,2,1536]{3,2,1,0:T(2,128)} %bitcast.98) | data formatting | bytes 3145728 | tf_op jit(solution)/shard_map/reshape;reshape;reshape;reshape | solution.py:245
  154.8 2.6 collective-permute-start.19
  157.3 9.4 %collective-permute-done.17 = f32[49408]{0:T(1024)S(1)} collective-permute-done((f32[49408]{0:T(1024)S(1)}, f32[49408]{0:T(1024)S(1)}, u32[]{:S(2)}, u32[]{:S(2)}) %collective-permute-start.17) | collective-permute-done | bytes 197664 | tf_op jit(solution)/shard_map/ppermute | solution.py:224
  174.0 7.4 %collective-permute-start.21 = (f32[12544]{0:T(1024)}, f32[12544]{0:T(1024)}, u32[]{:S(2)}, u32[]{:S(2)}) collective-permute-start(f32[12544]{0:T(1024)} %get-tuple-element.81), channel_id=1, source_target_pairs={{0,4},{1,5},{2,6},{3,7},{4,0},{5,1},{6,2},{7,3},{8,12},{9,13},{10,... | collective-permute-start | bytes 150536 | tf_op jit(solution)/shard_map/ppermute | solution.py:224
  193.0 6.1 %collective-permute-start.23 = (f32[6400]{0:T(1024)}, f32[6400]{0:T(1024)}, u32[]{:S(2)}, u32[]{:S(2)}) collective-permute-start(f32[6400]{0:T(1024)} %pad_maximum_fusion.10), channel_id=1, source_target_pairs={{0,32},{1,33},{2,34},{3,35},{4,36},{5,37},{6,38},{7,39},{8,40},{9,... | collective-permute-start | bytes 76808 | tf_op jit(solution)/shard_map/ppermute | solution.py:224
  200.4 4.8 %collective-permute-start.14 = (bf16[2,384,768]{2,1,0:T(8,128)(2,1)S(1)}, bf16[2,384,768]{2,1,0:T(8,128)(2,1)}, u32[]{:S(2)}, u32[]{:S(2)}) collective-permute-start(bf16[2,384,768]{2,1,0:T(8,128)(2,1)S(1)} %copy-done.13), channel_id=1, source_target_pairs={{1,0},{2,1},{3,2},{4,3},{5,4},{6,5},{7,6},{8,7},{9,8},{10,9},{11,1... | collective-permute-start | bytes 3538952 | tf_op jit(solution)/shard_map/ppermute | solution.py:224
  205.2 8.9 %collective-permute-start.15 = (bf16[2,384,768]{2,1,0:T(8,128)(2,1)S(1)}, bf16[2,384,768]{2,1,0:T(8,128)(2,1)}, u32[]{:S(2)}, u32[]{:S(2)}) collective-permute-start(bf16[2,384,768]{2,1,0:T(8,128)(2,1)S(1)} %copy-done.9), channel_id=1, source_target_pairs={{0,1},{1,2},{2,3},{3,4},{4,5},{5,6},{6,7},{7,8},{8,9},{9,10},{10,1... | collective-permute-start | bytes 3538952 | tf_op jit(solution)/shard_map/ppermute | solution.py:224
  216.0 11.8 %collective-permute-start.13 = (bf16[2,384,768]{2,1,0:T(8,128)(2,1)S(1)}, bf16[2,384,768]{2,1,0:T(8,128)(2,1)}, u32[]{:S(2)}, u32[]{:S(2)}) collective-permute-start(bf16[2,384,768]{2,1,0:T(8,128)(2,1)S(1)} %copy-done.11), channel_id=1, source_target_pairs={{0,1},{1,2},{2,3},{3,4},{4,5},{5,6},{6,7},{7,8},{8,9},{9,10},{10,1... | collective-permute-start | bytes 3538952 | tf_op jit(solution)/shard_map/ppermute | solution.py:224
  233.8 31.9 %collective-permute-done.26 = f32[256]{0:T(256)} collective-permute-done((f32[256]{0:T(256)}, f32[256]{0:T(256)}, u32[]{:S(2)}, u32[]{:S(2)}) %collective-permute-start.26) | collective-permute-done | bytes 1056 | tf_op jit(solution)/shard_map/ppermute | solution.py:301
  280.7 5.7 %shard_map.163 = (bf16[384,1536]{1,0:T(8,128)(2,1)}, bf16[384,1536]{1,0:T(8,128)(2,1)}) custom-call(bf16[384,1536]{1,0:T(8,128)(2,1)} %bitcast.80, f32[2,384,768]{2,1,0:T(8,128)} %copy-done.2, bf16[2,384,768]{2,1,0:T(8,128)(2,1)} %collective-permute-done.14.a_ref, bf16[2,384,768]{2,1,0:T(8,128)(2,1)} %collective-permute-done.15.b_ref, f32[1,128]{1,0:T(1,128)} %bitcast.87), custom_call_target="tpu_custom_call" | custom-call | flops 5898240 | bytes 6488064 | tf_op jit(solution)/shard_map/pallas_call | solution.py:212
  286.4 5.7 %shard_map.164 = (bf16[384,1536]{1,0:T(8,128)(2,1)}, bf16[384,1536]{1,0:T(8,128)(2,1)}) custom-call(bf16[384,1536]{1,0:T(8,128)(2,1)} %bitcast.81, f32[2,384,768]{2,1,0:T(8,128)} %copy-done.3, bf16[2,384,768]{2,1,0:T(8,128)(2,1)} %collective-permute-done.12.a_ref, ...), custom_call_target="tpu_custom_call", output_to_operand_aliasing={{0}: (5, {}), {1}: (6, {})} | custom-call | flops 5898240 | bytes 6488064 | tf_op jit(solution)/shard_map/pallas_call | solution.py:212
  (181 shorter events, 74.6 us)
Async XLA Ops:
  3.5 111.2 %collective-permute-start.1 = (bf16[2,384,768]{2,1,0:T(8,128)(2,1)}, bf16[2,384,768]{2,1,0:T(8,128)(2,1)}, u32[]{:S(2)}, u32[]{:S(2)}) collective-permute-start(bf16[2,384,768]{2,1,0:T(8,128)(2,1)} %pad_maximum_fusion.1), channel_id=1, source_target_pairs={{1,0},{2,1},{3,2},{4,3},{5,4},{6,5},{7,6},{8,7},{9,8},{10,9},{11,1... | collective-permute-start | bytes 3538952 | tf_op jit(solution)/shard_map/ppermute | solution.py:224
  6.1 108.6 %collective-permute-start = (bf16[2,384,768]{2,1,0:T(8,128)(2,1)}, bf16[2,384,768]{2,1,0:T(8,128)(2,1)}, u32[]{:S(2)}, u32[]{:S(2)}) collective-permute-start(bf16[2,384,768]{2,1,0:T(8,128)(2,1)} %pad_maximum_fusion.1), channel_id=1, source_target_pairs={{0,1},{1,2},{2,3},{3,4},{4,5},{5,6},{6,7},{7,8},{8,9},{9,10},{10,1... | collective-permute-start | bytes 3538952 | tf_op jit(solution)/shard_map/ppermute | solution.py:224
  18.4 67.8 %collective-permute-start.11 = (bf16[2,384,768]{2,1,0:T(8,128)(2,1)}, bf16[2,384,768]{2,1,0:T(8,128)(2,1)}, u32[]{:S(2)}, u32[]{:S(2)}) collective-permute-start(bf16[2,384,768]{2,1,0:T(8,128)(2,1)} %pad_maximum_fusion.2), channel_id=1, source_target_pairs={{1,0},{2,1},{3,2},{4,3},{5,4},{6,5},{7,6},{8,7},{9,8},{10,9},{11,1... | collective-permute-start | bytes 3538952 | tf_op jit(solution)/shard_map/ppermute | solution.py:224
  20.3 65.9 %collective-permute-start.10 = (bf16[2,384,768]{2,1,0:T(8,128)(2,1)}, bf16[2,384,768]{2,1,0:T(8,128)(2,1)}, u32[]{:S(2)}, u32[]{:S(2)}) collective-permute-start(bf16[2,384,768]{2,1,0:T(8,128)(2,1)} %pad_maximum_fusion.2), channel_id=1, source_target_pairs={{0,1},{1,2},{2,3},{3,4},{4,5},{5,6},{6,7},{7,8},{8,9},{9,10},{10,1... | collective-permute-start | bytes 3538952 | tf_op jit(solution)/shard_map/ppermute | solution.py:224
  38.0 4.5 %collective-permute-start.4 = (bf16[2,48,128]{2,1,0:T(8,128)(2,1)S(1)}, bf16[2,48,128]{2,1,0:T(8,128)(2,1)S(1)}, u32[]{:S(2)}, u32[]{:S(2)}) collective-permute-start(bf16[2,48,128]{2,1,0:T(8,128)(2,1)S(1)} %get-tuple-element.72), channel_id=1, source_target_pairs={{0,4},{1,5},{2,6},{3,7},{4,0},{5,1},{6,2},{7,3},{8,12},{9,13},{10,... | collective-permute-start | bytes 73736 | tf_op jit(solution)/shard_map/ppermute | solution.py:224
  42.5 4.3 %collective-permute-start.5 = (bf16[2,48,128]{2,1,0:T(8,128)(2,1)S(1)}, bf16[2,48,128]{2,1,0:T(8,128)(2,1)S(1)}, u32[]{:S(2)}, u32[]{:S(2)}) collective-permute-start(bf16[2,48,128]{2,1,0:T(8,128)(2,1)S(1)} %get-tuple-element.72), channel_id=1, source_target_pairs={{0,6},{1,7},{2,0},{3,1},{4,2},{5,3},{6,4},{7,5},{8,14},{9,15},{10,... | collective-permute-start | bytes 73736 | tf_op jit(solution)/shard_map/ppermute | solution.py:224
  50.3 5.0 %collective-permute-start.7 = (bf16[8,48,128]{2,1,0:T(8,128)(2,1)S(1)}, bf16[8,48,128]{2,1,0:T(8,128)(2,1)S(1)}, u32[]{:S(2)}, u32[]{:S(2)}) collective-permute-start(bf16[8,48,128]{2,1,0:T(8,128)(2,1)S(1)} %get-tuple-element.65), channel_id=1, source_target_pairs={{0,16},{1,17},{2,18},{3,19},{4,20},{5,21},{6,22},{7,23},{8,24},{9,... | collective-permute-start | bytes 294920 | tf_op jit(solution)/shard_map/ppermute | solution.py:224
  55.3 4.7 %collective-permute-start.8 = (bf16[8,48,128]{2,1,0:T(8,128)(2,1)S(1)}, bf16[8,48,128]{2,1,0:T(8,128)(2,1)S(1)}, u32[]{:S(2)}, u32[]{:S(2)}) collective-permute-start(bf16[8,48,128]{2,1,0:T(8,128)(2,1)S(1)} %get-tuple-element.65), channel_id=1, source_target_pairs={{0,24},{1,25},{2,26},{3,27},{4,28},{5,29},{6,30},{7,31},{8,0},{9,1... | collective-permute-start | bytes 294920 | tf_op jit(solution)/shard_map/ppermute | solution.py:224
  59.9 22.0 %collective-permute-start.9 = (bf16[32,48,128]{2,1,0:T(8,128)(2,1)S(1)}, bf16[32,48,128]{2,1,0:T(8,128)(2,1)S(1)}, u32[]{:S(2)}, u32[]{:S(2)}) collective-permute-start(bf16[32,48,128]{2,1,0:T(8,128)(2,1)S(1)} %constant_dynamic-update-slice_fusion.9), channel_id=1, source_target_pairs={{0,32},{1,33},{2,34},{3,35},{4,36},{5,37},{6,38},{7,39},{8,40},{9,... | collective-permute-start | bytes 1179656 | tf_op jit(solution)/shard_map/ppermute | solution.py:224
  149.1 3.6 %collective-permute-start.16 = (f32[196864]{0:T(1024)S(1)}, f32[196864]{0:T(1024)S(1)}, u32[]{:S(2)}, u32[]{:S(2)}) collective-permute-start(f32[196864]{0:T(1024)S(1)} %pad_maximum_fusion.3), channel_id=1, source_target_pairs={{0,1},{1,0},{2,3},{3,2},{4,5},{5,4},{6,7},{7,6},{8,9},{9,8},{10,11... | collective-permute-start | bytes 2362376 | tf_op jit(solution)/shard_map/ppermute | solution.py:224
  154.6 12.1 %collective-permute-start.17 = (f32[49408]{0:T(1024)S(1)}, f32[49408]{0:T(1024)S(1)}, u32[]{:S(2)}, u32[]{:S(2)}) collective-permute-start(f32[49408]{0:T(1024)S(1)} %get-tuple-element.83), channel_id=1, source_target_pairs={{0,24},{1,25},{2,26},{3,27},{4,28},{5,29},{6,30},{7,31},{8,0},{9,1... | collective-permute-start | bytes 592904 | tf_op jit(solution)/shard_map/ppermute | solution.py:224
  154.7 13.5 %collective-permute-start.18 = (f32[49408]{0:T(1024)S(1)}, f32[49408]{0:T(1024)S(1)}, u32[]{:S(2)}, u32[]{:S(2)}) collective-permute-start(f32[49408]{0:T(1024)S(1)} %get-tuple-element.84), channel_id=1, source_target_pairs={{0,16},{1,17},{2,18},{3,19},{4,20},{5,21},{6,22},{7,23},{8,24},{9,... | collective-permute-start | bytes 592904 | tf_op jit(solution)/shard_map/ppermute | solution.py:224
  154.8 14.2 %collective-permute-start.19 = (f32[49408]{0:T(1024)S(1)}, f32[49408]{0:T(1024)S(1)}, u32[]{:S(2)}, u32[]{:S(2)}) collective-permute-start(f32[49408]{0:T(1024)S(1)} %get-tuple-element.85), channel_id=1, source_target_pairs={{0,8},{1,9},{2,10},{3,11},{4,12},{5,13},{6,14},{7,15},{8,16},{9,17... | collective-permute-start | bytes 592904 | tf_op jit(solution)/shard_map/ppermute | solution.py:224
  174.0 7.7 %collective-permute-start.20 = (f32[12544]{0:T(1024)S(1)}, f32[12544]{0:T(1024)S(1)}, u32[]{:S(2)}, u32[]{:S(2)}) collective-permute-start(f32[12544]{0:T(1024)S(1)} %get-tuple-element.80), channel_id=1, source_target_pairs={{0,6},{1,7},{2,0},{3,1},{4,2},{5,3},{6,4},{7,5},{8,14},{9,15},{10,... | collective-permute-start | bytes 150536 | tf_op jit(solution)/shard_map/ppermute | solution.py:224
  174.0 10.4 %collective-permute-start.21 = (f32[12544]{0:T(1024)}, f32[12544]{0:T(1024)}, u32[]{:S(2)}, u32[]{:S(2)}) collective-permute-start(f32[12544]{0:T(1024)} %get-tuple-element.81), channel_id=1, source_target_pairs={{0,4},{1,5},{2,6},{3,7},{4,0},{5,1},{6,2},{7,3},{8,12},{9,13},{10,... | collective-permute-start | bytes 150536 | tf_op jit(solution)/shard_map/ppermute | solution.py:224
  181.4 5.9 %collective-permute-start.22 = (f32[12544]{0:T(1024)}, f32[12544]{0:T(1024)}, u32[]{:S(2)}, u32[]{:S(2)}) collective-permute-start(f32[12544]{0:T(1024)} %get-tuple-element.82), channel_id=1, source_target_pairs={{0,2},{1,3},{2,4},{3,5},{4,6},{5,7},{6,0},{7,1},{8,10},{9,11},{10,... | collective-permute-start | bytes 150536 | tf_op jit(solution)/shard_map/ppermute | solution.py:224
  193.0 34.8 %collective-permute-start.23 = (f32[6400]{0:T(1024)}, f32[6400]{0:T(1024)}, u32[]{:S(2)}, u32[]{:S(2)}) collective-permute-start(f32[6400]{0:T(1024)} %pad_maximum_fusion.10), channel_id=1, source_target_pairs={{0,32},{1,33},{2,34},{3,35},{4,36},{5,37},{6,38},{7,39},{8,40},{9,... | collective-permute-start | bytes 76808 | tf_op jit(solution)/shard_map/ppermute | solution.py:224
  200.4 80.3 %collective-permute-start.14 = (bf16[2,384,768]{2,1,0:T(8,128)(2,1)S(1)}, bf16[2,384,768]{2,1,0:T(8,128)(2,1)}, u32[]{:S(2)}, u32[]{:S(2)}) collective-permute-start(bf16[2,384,768]{2,1,0:T(8,128)(2,1)S(1)} %copy-done.13), channel_id=1, source_target_pairs={{1,0},{2,1},{3,2},{4,3},{5,4},{6,5},{7,6},{8,7},{9,8},{10,9},{11,1... | collective-permute-start | bytes 3538952 | tf_op jit(solution)/shard_map/ppermute | solution.py:224
  205.2 75.4 %collective-permute-start.15 = (bf16[2,384,768]{2,1,0:T(8,128)(2,1)S(1)}, bf16[2,384,768]{2,1,0:T(8,128)(2,1)}, u32[]{:S(2)}, u32[]{:S(2)}) collective-permute-start(bf16[2,384,768]{2,1,0:T(8,128)(2,1)S(1)} %copy-done.9), channel_id=1, source_target_pairs={{0,1},{1,2},{2,3},{3,4},{4,5},{5,6},{6,7},{7,8},{8,9},{9,10},{10,1... | collective-permute-start | bytes 3538952 | tf_op jit(solution)/shard_map/ppermute | solution.py:224
  214.1 72.3 %collective-permute-start.12 = (bf16[2,384,768]{2,1,0:T(8,128)(2,1)}, bf16[2,384,768]{2,1,0:T(8,128)(2,1)}, u32[]{:S(2)}, u32[]{:S(2)}) collective-permute-start(bf16[2,384,768]{2,1,0:T(8,128)(2,1)} %copy-done.14), channel_id=1, source_target_pairs={{1,0},{2,1},{3,2},{4,3},{5,4},{6,5},{7,6},{8,7},{9,8},{10,9},{11,1... | collective-permute-start | bytes 3538952 | tf_op jit(solution)/shard_map/ppermute | solution.py:224
  216.0 70.3 %collective-permute-start.13 = (bf16[2,384,768]{2,1,0:T(8,128)(2,1)S(1)}, bf16[2,384,768]{2,1,0:T(8,128)(2,1)}, u32[]{:S(2)}, u32[]{:S(2)}) collective-permute-start(bf16[2,384,768]{2,1,0:T(8,128)(2,1)S(1)} %copy-done.11), channel_id=1, source_target_pairs={{0,1},{1,2},{2,3},{3,4},{4,5},{5,6},{6,7},{7,8},{8,9},{9,10},{10,1... | collective-permute-start | bytes 3538952 | tf_op jit(solution)/shard_map/ppermute | solution.py:224
  229.0 36.7 %collective-permute-start.26 = (f32[256]{0:T(256)}, f32[256]{0:T(256)}, u32[]{:S(2)}, u32[]{:S(2)}) collective-permute-start(f32[256]{0:T(256)} %slice_add_fusion.1), channel_id=1, source_target_pairs={{0,192},{64,0},{128,64},{192,128},{1,193},{65,1},{129,65},{193,129... | collective-permute-start | bytes 3080 | tf_op jit(solution)/shard_map/ppermute | solution.py:301
  265.8 9.3 %collective-permute-start.25 = (f32[256]{0:T(256)}, f32[256]{0:T(256)}, u32[]{:S(2)}, u32[]{:S(2)}) collective-permute-start(f32[256]{0:T(256)} %slice_add_fusion.1), channel_id=1, source_target_pairs={{0,128},{64,192},{128,0},{192,64},{1,129},{65,193},{129,1},{193,65... | collective-permute-start | bytes 3080 | tf_op jit(solution)/shard_map/ppermute | solution.py:301
  275.0 4.4 %collective-permute-start.24 = (f32[256]{0:T(256)}, f32[256]{0:T(256)S(1)}, u32[]{:S(2)}, u32[]{:S(2)}) collective-permute-start(f32[256]{0:T(256)} %slice_add_fusion.1), channel_id=1, source_target_pairs={{0,64},{64,128},{128,192},{192,0},{1,65},{65,129},{129,193},{193,1... | collective-permute-start | bytes 3080 | tf_op jit(solution)/shard_map/ppermute | solution.py:301
  (29 other events, 244.3 us)
